TPU v7x, 32 devices: a whole 2x2x4 slice. The times are simulated.
32 devices in a mesh: seq: 8 (over y, x, core), head: 4 (over z).
Axes of the slice: x: 2, y: 2, z: 4, core: 2. Of those that a mesh axis runs over, the one named last changes fastest.
Arguments:
- queries: bfloat16 [4096, 4096], P(('seq', 'head')), may hold values from -6 to 6
- keys: bfloat16 [4096, 4096], P(('seq', 'head')), may hold values from -6 to 6
- values: bfloat16 [4096, 4096], P(('seq', 'head')), may hold values from -6 to 6
- beta: bfloat16 [4096, 32], P(('seq', 'head')), may hold values from 0 to 1
- log_decay: bfloat16 [4096, 32], P(('seq', 'head')), may hold values from -1 to 0
- seg_lengths: int32 [8], replicated, may hold values from 1 to 3072, 4096 in all
Outputs:
- mixed: bfloat16 [4096, 4096], P(('seq', 'head'))
All inputs are finite; a program needn't handle non-finite values.
Results may differ from a plain program's by a relative error of at most 0.0017.
Values may be sent and summed in bfloat16 or wider, within the bound.
A program may use at most 128 MiB of HBM per device.

v0:
```python
from functools import partial

import jax
import jax.numpy as jnp
from jax import lax
from jax.sharding import PartitionSpec as P

DK = 128
DV = 128
SPAN = 64


def span_parts(query_rows, key_rows, value_rows, write_rate, log_gate, reset_flags, inclusive):
    highest = lax.Precision.HIGHEST
    block_rows = query_rows.shape[0]
    log_level = jnp.cumsum(log_gate)
    region = jnp.cumsum(reset_flags)
    row_indices = jnp.arange(block_rows)[:, None]
    col_ids = jnp.arange(block_rows)[None, :]
    inside_segment_mask = (col_ids <= row_indices) & (region[:, None] == region[None, :])
    log_gap = jnp.where(inside_segment_mask, log_level[:, None] - log_level[None, :], 0.0)
    weight = jnp.where(inside_segment_mask, jnp.exp(log_gap), 0.0)
    carried = jnp.where(region == 0, jnp.exp(log_level), 0.0)
    strictly = col_ids < row_indices
    intersection = jnp.dot(key_rows, key_rows.T, precision=highest)
    system = jnp.eye(block_rows, dtype=query_rows.dtype) + jnp.where(
        strictly, write_rate[:, None] * weight * intersection, 0.0
    )
    right_side = jnp.concatenate(
        [write_rate[:, None] * value_rows, (write_rate * carried)[:, None] * key_rows], axis=1
    )
    solved = jax.scipy.linalg.solve_triangular(system, right_side, lower=True, unit_diagonal=True)
    value_width = value_rows.shape[1]
    update = solved[:, :value_width]
    shrink = solved[:, value_width:]
    scores = jnp.dot(query_rows, key_rows.T, precision=highest) * weight
    if not inclusive:
        scores = jnp.where(strictly, scores, 0.0)
    local_out = jnp.dot(scores, update, precision=highest)
    effective = carried[:, None] * query_rows - jnp.dot(scores, shrink, precision=highest)
    trailing_weight = weight[block_rows - 1]
    scaled = trailing_weight[:, None] * key_rows
    transit = carried[block_rows - 1] * jnp.eye(
        key_rows.shape[1], dtype=query_rows.dtype
    ) - jnp.dot(shrink.T, scaled, precision=highest)
    inject = jnp.dot(update.T, scaled, precision=highest)
    return (local_out, effective, transit, inject)


def block_pieces(query_rows, key_rows, value_rows, write_rate, log_gate, reset_flags, inclusive):
    count = query_rows.shape[0] // SPAN

    def split(member):
        return member.reshape((count, SPAN) + member.shape[1:])

    return jax.vmap(partial(span_parts, inclusive=inclusive))(
        split(query_rows),
        split(key_rows),
        split(value_rows),
        split(write_rate),
        split(log_gate),
        split(reset_flags),
    )


def combine(earlier, later):
    highest = lax.Precision.HIGHEST
    return (
        jnp.einsum("hij,hjk->hik", earlier[0], later[0], precision=highest),
        jnp.einsum("hij,hjk->hik", earlier[1], later[0], precision=highest) + later[1],
    )


def summarize(transit, inject):
    heads = transit.shape[0]
    start = (
        jnp.broadcast_to(jnp.eye(DK, dtype=jnp.float32), (heads, DK, DK)),
        jnp.zeros((heads, DV, DK), jnp.float32),
    )

    def step(carry, piece):
        return (combine(carry, piece), None)

    result, unused = lax.scan(
        step, start, (jnp.moveaxis(transit, 1, 0), jnp.moveaxis(inject, 1, 0))
    )
    return result


def emit(local_out, effective, transit, inject, state):
    highest = lax.Precision.HIGHEST
    moved = (
        jnp.moveaxis(local_out, 1, 0),
        jnp.moveaxis(effective, 1, 0),
        jnp.moveaxis(transit, 1, 0),
        jnp.moveaxis(inject, 1, 0),
    )

    def step(carry, piece):
        out_block, effect_rows, transit_step, inject_step = piece
        produced = out_block + jnp.einsum("hck,hvk->hcv", effect_rows, carry, precision=highest)
        carry = jnp.einsum("hvj,hjk->hvk", carry, transit_step, precision=highest) + inject_step
        return (carry, produced)

    final_state, produced = lax.scan(step, state, moved)
    heads = produced.shape[1]
    return jnp.moveaxis(produced, 0, 1).reshape(heads, -1, produced.shape[-1])


def on_device(queries, keys, values, beta, log_decay, seg_lengths):
    highest = lax.Precision.HIGHEST
    query_all, key_all, value_all, rate_all, gate_values_full = (
        lax.all_to_all(queries, "head", split_axis=1, concat_axis=0, tiled=True),
        lax.all_to_all(keys, "head", split_axis=1, concat_axis=0, tiled=True),
        lax.all_to_all(values, "head", split_axis=1, concat_axis=0, tiled=True),
        lax.all_to_all(beta, "head", split_axis=1, concat_axis=0, tiled=True),
        lax.all_to_all(log_decay, "head", split_axis=1, concat_axis=0, tiled=True),
    )
    rows = query_all.shape[0]
    heads = rate_all.shape[1]
    spread = lax.axis_size("seq")
    place = lax.axis_index("seq")
    total = rows * spread
    starts = jnp.cumsum(seg_lengths) - seg_lengths
    positions = place * rows + jnp.arange(rows, dtype=jnp.int32)
    forward_reset = jnp.any(positions[:, None] == starts[None, :], axis=1).astype(jnp.int32)
    backward_reset = (
        jnp.any((positions + 1)[:, None] == starts[None, :], axis=1) | (positions == total - 1)
    ).astype(jnp.int32)

    def by_head(array, width):
        return array.reshape(rows, heads, width).transpose(1, 0, 2).astype(jnp.float32)

    query_heads = by_head(query_all, DK)
    key_raw = by_head(key_all, DK)
    key_heads = key_raw / jnp.sqrt(jnp.sum(key_raw * key_raw, axis=-1, keepdims=True) + 1e-06)
    value_heads = by_head(value_all, DV)
    rate_heads = rate_all.T.astype(jnp.float32)
    gate_heads = gate_values_full.T.astype(jnp.float32)
    forward_pieces = jax.vmap(partial(block_pieces, reset_flags=forward_reset, inclusive=True))(
        query_heads, key_heads, value_heads, rate_heads, gate_heads
    )
    backward_pieces = jax.vmap(
        partial(block_pieces, reset_flags=backward_reset[::-1], inclusive=False)
    )(
        query_heads[:, ::-1],
        key_heads[:, ::-1],
        value_heads[:, ::-1],
        rate_heads[:, ::-1],
        gate_heads[:, ::-1],
    )
    forward_sum = summarize(forward_pieces[2], forward_pieces[3])
    backward_sum = summarize(backward_pieces[2], backward_pieces[3])
    every = (
        lax.all_gather(forward_sum[0][None], "seq", axis=0, tiled=True),
        lax.all_gather(forward_sum[1][None], "seq", axis=0, tiled=True),
        lax.all_gather(backward_sum[0][None], "seq", axis=0, tiled=True),
        lax.all_gather(backward_sum[1][None], "seq", axis=0, tiled=True),
    )
    empty = jnp.zeros_like(forward_sum[1])

    def take_lower(step, state):
        moved = (
            jnp.einsum("hvj,hjk->hvk", state, every[0][step], precision=highest) + every[1][step]
        )
        return jnp.where(step < place, moved, state)

    def take_upper(step, state):
        source = spread - 1 - step
        moved = (
            jnp.einsum("hvj,hjk->hvk", state, every[2][source], precision=highest)
            + every[3][source]
        )
        return jnp.where(source > place, moved, state)

    forward_in = lax.fori_loop(0, spread, take_lower, empty)
    backward_in = lax.fori_loop(0, spread, take_upper, empty)
    forward_out = emit(
        forward_pieces[0], forward_pieces[1], forward_pieces[2], forward_pieces[3], forward_in
    )
    backward_out = emit(
        backward_pieces[0], backward_pieces[1], backward_pieces[2], backward_pieces[3], backward_in
    )[:, ::-1]
    mixed = (
        (forward_out + backward_out)
        .transpose(1, 0, 2)
        .reshape(rows, heads * DV)
        .astype(jnp.bfloat16)
    )
    return lax.all_to_all(mixed, "head", split_axis=0, concat_axis=1, tiled=True)


def solution(mesh):
    in_specs = (
        P(("seq", "head"), None),
        P(("seq", "head"), None),
        P(("seq", "head"), None),
        P(("seq", "head"), None),
        P(("seq", "head"), None),
        P(),
    )
    out_specs = P(("seq", "head"), None)
    return jax.shard_map(
        on_device, mesh=mesh, in_specs=in_specs, out_specs=out_specs, check_vma=False
    )
```

profile of v0, /device:TPU:0, one launch (start us, length us, event | category | flops | bytes accessed | tf_op | source)
XLA Modules:
  0.0 1090.1 jit_solution(6707808638784264587)
XLA Ops:
  6.5 6.3 all-to-all-start
  36.4 17.8 %all-to-all-done.2 = bf16[128,4,1024]{2,0,1:T(8,128)(2,1)S(1)} async-done(((bf16[128,4,1024]{2,0,1:T(8,128)(2,1)}), bf16[128,4,1024]{2,0,1:T(8,128)(2,1)S(1)}, u32[]{:S(2)}, u32[]{:S(2)}) %all-to-all-start.2) | async-done | bytes 1048608 | tf_op jit(solution)/shard_map/all_to_all | solution.py:114
  68.1 316.0 %custom-call.8 = f32[8,8,1,64,64]{3,4,2,1,0:T(8,128)} custom-call(f32[8,8,1,64,64]{4,3,2,1,0:T(8,128)} %add_bitcast_fusion.1), custom_call_target="InvertDiagBlocksLowerTriangular" | custom-call | tf_op jit(solution)/shard_map/vmap(vmap(jit(_solve_triangular)))/triangular_solve | solution.py:32
  395.4 9.2 convolution_bitcast_fusion.9
  404.6 9.5 bitcast_subtract_fusion.1
  414.1 5.3 copy.187
  419.5 5.5 copy.188
  425.0 29.4 %while.82 = (s32[]{:T(128)}, f32[8,128,128]{1,2,0:T(8,128)S(1)}, f32[8,128,128]{1,2,0:T(8,128)S(1)}, f32[8,8,128,128]{2,3,1,0:T(8,128)}, f32[8,8,128,128]{2,3,1,0:T(8,128)}, /*index=5*/s32[]{:T(128)}, s32[]{:T(128)}) while((s32[]{:T(128)}, f32[8,128,128]{1,2,0:T(8,128)S(1)}, f32[8,128,128]{1,2,0:T(8,128)S(1)}, ...), condition=%wide.region_6.8_spmd.clone, body=%wide.region_5.7_spmd.clone.sunk | while | flops 402915328 | bytes 5768791 | solution.py:84
  467.1 4.9 add_bitcast_fusion
  472.0 316.0 %custom-call.9 = f32[8,8,1,64,64]{3,4,2,1,0:T(8,128)} custom-call(f32[8,8,1,64,64]{4,3,2,1,0:T(8,128)} %add_bitcast_fusion), custom_call_target="InvertDiagBlocksLowerTriangular" | custom-call | tf_op jit(solution)/shard_map/vmap(vmap(jit(_solve_triangular)))/triangular_solve | solution.py:32
  798.0 9.6 bitcast_subtract_fusion
  807.7 5.4 copy.205
  813.0 10.2 convolution_bitcast_fusion.8
  823.2 5.3 copy.206
  828.6 29.4 %while.84 = (s32[]{:T(128)}, f32[8,128,128]{1,2,0:T(8,128)S(1)}, f32[8,128,128]{1,2,0:T(8,128)S(1)}, f32[8,8,128,128]{2,3,1,0:T(8,128)}, f32[8,8,128,128]{2,3,1,0:T(8,128)}, /*index=5*/s32[]{:T(128)}, s32[]{:T(128)}) while((s32[]{:T(128)}, f32[8,128,128]{1,2,0:T(8,128)S(1)}, f32[8,128,128]{1,2,0:T(8,128)S(1)}, ...), condition=%wide.region_15.17_spmd.clone, body=%wide.region_14.16_spmd.clone.sunk | while | flops 402915328 | bytes 5768791 | solution.py:84
  860.5 5.0 all-to-all-start.4
  865.5 24.7 %all-to-all-done.4 = bf16[128,4,1024]{2,0,1:T(8,128)(2,1)S(1)} async-done(((bf16[128,4,1024]{2,0,1:T(8,128)(2,1)}), bf16[128,4,1024]{2,0,1:T(8,128)(2,1)S(1)}, u32[]{:S(2)}, u32[]{:S(2)}) %all-to-all-start.4) | async-done | bytes 1048608 | tf_op jit(solution)/shard_map/all_to_all | solution.py:113
  920.7 5.4 fusion.94
  926.1 27.5 %while.83 = (s32[]{:T(128)}, f32[8,128,128]{1,2,0:T(8,128)S(1)}, s32[]{:T(128)}, f32[8,8,128,128]{3,2,1,0:T(8,128)}, f32[8,8,128,128]{3,2,1,0:T(8,128)}, /*index=5*/s32[]{:T(128)}, s32[]{:T(128)}) while((s32[]{:T(128)}, f32[8,128,128]{1,2,0:T(8,128)S(1)}, s32[]{:T(128)}, f32[8,8,128,128]{3,2,1,0:T(8,128)}, ...), condition=%wide.region_8.10_spmd.clone, body=%wide.region_7.9_spmd.clone.sunk | while | flops 201850880 | bytes 5769315 | solution.py:176
  953.9 28.5 %while.80 = (s32[]{:T(128)}, f32[8,128,128]{1,2,0:T(8,128)S(1)}, f32[8,8,64,128]{3,2,0,1:T(8,128)S(1)}, f32[8,8,128,128]{2,3,1,0:T(8,128)}, f32[8,8,128,128]{2,3...) while((s32[]{:T(128)}, f32[8,128,128]{1,2,0:T(8,128)S(1)}, ...), condition=%wide.region_10.12_spmd, body=%wide.region_9.11_spmd.sunk | while | flops 302186496 | bytes 4458581 | solution.py:105
  983.7 27.4 %while.85 = (s32[]{:T(128)}, f32[8,128,128]{1,2,0:T(8,128)S(1)}, s32[]{:T(128)}, f32[8,8,128,128]{3,2,1,0:T(8,128)}, f32[8,8,128,128]{3,2,1,0:T(8,128)}, /*index=5*/s32[]{:T(128)}, s32[]{:T(128)}, s32[]{:T(128)}, s32[]{:T(128)}) while((s32[]{:T(128)}, f32[8,128,128]{1,2,0:T(8,128)S(1)}, s32[]{:T(128)}, ...), condition=%wide.region_17.19_spmd.clone, body=%wide.region_16.18_spmd.clone.sunk | while | flops 201850880 | bytes 5769377 | solution.py:177
  1011.4 28.5 %while.81 = (s32[]{:T(128)}, f32[8,128,128]{1,2,0:T(8,128)S(1)}, f32[8,8,64,128]{3,2,0,1:T(8,128)S(1)}, f32[8,8,128,128]{2,3,1,0:T(8,128)}, f32[8,8,128,128]{2,3...) while((s32[]{:T(128)}, f32[8,128,128]{1,2,0:T(8,128)S(1)}, ...), condition=%wide.region_19.21_spmd, body=%wide.region_18.20_spmd.sunk | while | flops 302186496 | bytes 4458581 | solution.py:105
  1039.8 10.2 rev.27
  1053.7 27.5 %all_to_all.84 = bf16[4,128,1024]{2,1,0:T(8,128)(2,1)S(1)} all-to-all(bf16[4,128,1024]{2,1,0:T(8,128)(2,1)S(1)} %convert_element_type.121), channel_id=1, replica_groups=mesh['seq'=8,'head'=4] {'head'}, dimensions={0} | all-to-all | bytes 2097152 | tf_op jit(solution)/shard_map/all_to_all | solution.py:190
  (325 shorter events, 279.9 us)
Async XLA Ops:
  6.5 11.9 %all-to-all-start = ((bf16[128,4,8]{0,2,1:T(8,128)(2,1)}), bf16[128,4,8]{0,2,1:T(8,128)(2,1)S(1)}, u32[]{:S(2)}, u32[]{:S(2)}) async-start(bf16[128,4,8]{0,2,1:T(8,128)(2,1)} %bitcast.338), calls=%async_computation | async-start | bytes 16384 | tf_op jit(solution)/shard_map/all_to_all | solution.py:117
  18.4 8.8 all-to-all-start.1
  21.7 9.5 copy-start.19
  27.3 26.9 %all-to-all-start.2 = ((bf16[128,4,1024]{2,0,1:T(8,128)(2,1)}), bf16[128,4,1024]{2,0,1:T(8,128)(2,1)S(1)}, u32[]{:S(2)}, u32[]{:S(2)}) async-start(bf16[128,4,1024]{2,0,1:T(8,128)(2,1)} %bitcast.229), calls=%async_computation.2 | async-start | bytes 2097152 | tf_op jit(solution)/shard_map/all_to_all | solution.py:114
  54.2 331.8 %all-to-all-start.3 = ((bf16[128,4,1024]{2,0,1:T(8,128)(2,1)}), bf16[128,4,1024]{2,0,1:T(8,128)(2,1)}, u32[]{:S(2)}, u32[]{:S(2)}) async-start(bf16[128,4,1024]{2,0,1:T(8,128)(2,1)} %bitcast.228), calls=%async_computation.3 | async-start | bytes 2097152 | tf_op jit(solution)/shard_map/all_to_all | solution.py:115
  58.4 867.7 %all-gather.9.cloned.1.call-start = ((), (), s32[]{:S(2)}) async-start(), calls=%async_computation.6 | async-start | bytes 4718592 | tf_op jit(solution)/shard_map/all_gather | solution.py:155
  62.4 342.2 %copy-start = (f32[8,512,128]{2,1,0:T(8,128)}, f32[8,512,128]{2,1,0:T(8,128)S(1)}, u32[]{:S(2)}) copy-start(f32[8,512,128]{2,1,0:T(8,128)S(1)} %copy.182) | copy-start | bytes 6291460
  389.4 1.6 copy-start.12
  389.4 2.2 copy-start.17
  395.4 9.2 copy-start.4
  455.4 470.7 %all-gather.11.cloned.1.call-start = ((), (), s32[]{:S(2)}) async-start(), calls=%async_computation.7 | async-start | bytes 4718592 | tf_op jit(solution)/shard_map/all_gather | solution.py:156
  455.5 4.9 copy-start.9
  456.6 525.8 %all-gather.13.cloned.1.call-start = ((), (), s32[]{:S(2)}) async-start(), calls=%async_computation.8 | async-start | bytes 4718592 | tf_op jit(solution)/shard_map/all_gather | solution.py:157
  467.1 346.0 %copy-start.2 = (f32[8,512,128]{2,1,0:T(8,128)}, f32[8,512,128]{2,1,0:T(8,128)S(1)}, u32[]{:S(2)}) copy-start(f32[8,512,128]{2,1,0:T(8,128)S(1)} %copy.202) | copy-start | bytes 6291460
  790.6 1.6 copy-start.18
  796.0 2.1 copy-start.6
  860.5 29.7 %all-to-all-start.4 = ((bf16[128,4,1024]{2,0,1:T(8,128)(2,1)}), bf16[128,4,1024]{2,0,1:T(8,128)(2,1)S(1)}, u32[]{:S(2)}, u32[]{:S(2)}) async-start(bf16[128,4,1024]{2,0,1:T(8,128)(2,1)} %bitcast.227), calls=%async_computation.4 | async-start | bytes 2097152 | tf_op jit(solution)/shard_map/all_to_all | solution.py:113
  865.5 116.9 %all-gather.15.cloned.1.call-start = ((), (), s32[]{:S(2)}) async-start(), calls=%async_computation.9 | async-start | bytes 4718592 | tf_op jit(solution)/shard_map/all_gather | solution.py:158
  901.2 2.2 copy-start.1
  901.2 2.5 copy-start.16
  903.7 2.4 copy-start.5
  906.1 3.6 copy-start.3
  909.6 3.6 copy-start.14
  913.2 3.7 copy-start.7
  (6 other events, 7.7 us)
Sparse Core Ops, SparseCore 0:
  455.6 38.5 all-gather.8
  496.0 37.0 all-gather.10
  859.2 38.0 all-gather.12
  920.8 35.7 all-gather.14
where the time goes:
time: 1100 us; the launch traced here: 1090 us
  other arithmetic  650 us (59%)
  matrix products  224 us (20%)
  local copies, waits for them, and re-layouts  101 us (9%)
  waiting for transfers between devices  49.4 us (4%)
  blocking collectives  27.5 us (2%)
  starting transfers between devices  22.5 us (2%)
  between operations  14.1 us (1%)
    another operation x4, other arithmetic, span_parts(): jax.scipy.linalg.solve_triangular(system, right_side, lower=True, unit_di...  632 us
    unnamed x49, local copies, waits for them, and re-layouts  34.7 us
    dot_general x16, matrix products, step(): jnp.einsum('hvj,hjk->hvk', carry, transit_step, precision=highest)  29.6 us
    dot_general x16, matrix products, combine(): jnp.einsum('hij,hjk->hik', earlier[1], later[0], precision=highest)  29.6 us
    all_to_all x1, blocking collectives, on_device(): lax.all_to_all(mixed, 'head', split_axis=0, concat_axis=1, tiled=True)  27.5 us
    dot_general x16, matrix products, combine(): jnp.einsum('hij,hjk->hik', earlier[0], later[0], precision=highest)  27.4 us
    dot_general x16, matrix products, step(): jnp.einsum('hck,hvk->hcv', effect_rows, carry, precision=highest)  26.1 us
    all_to_all x1, waiting for transfers between devices, on_device(): lax.all_to_all(queries, 'head', split_axis=1, concat_axis=0, tiled=True)  24.7 us
  transfers between devices with their start and end apart: 9, of which 4 were waited for; matrix products, arithmetic and copies ran while one was open for 76% of the time, Pallas kernels for 0%

commit v1 on v0

--- a/solution.py
+++ b/solution.py
@@ -3,11 +3,237 @@
 import jax
 import jax.numpy as jnp
 from jax import lax
+from jax.experimental import pallas as pl
+from jax.experimental.pallas import tpu as pltpu
 from jax.sharding import PartitionSpec as P
 
 DK = 128
 DV = 128
 SPAN = 64
+TILE = 128
+SIDE = 16
+GROUP = 4
+LEVELS = 6
+
+
+def mm(a, b):
+    return jnp.dot(a, b, preferred_element_type=jnp.float32)
+
+
+def halves(a):
+    high = a.astype(jnp.bfloat16)
+    low = (a - high.astype(jnp.float32)).astype(jnp.bfloat16)
+    return high, low
+
+
+def wide(a):
+    return jnp.concatenate(halves(a), axis=1)
+
+
+def right(high, low):
+    row = jnp.concatenate([high, low], axis=1)
+    return jnp.concatenate([row, row], axis=0)
+
+
+def fold(a):
+    return a[:, :TILE] + a[:, TILE:]
+
+
+def mix_kernel(count, group, lengths, x_ref, out_ref, masks, fe, go, partial_out):
+    bf16, f32 = jnp.bfloat16, jnp.float32
+    rows = lax.broadcasted_iota(jnp.int32, (TILE, TILE), 0)
+    cols = lax.broadcasted_iota(jnp.int32, (TILE, TILE), 1)
+    rows_w = lax.broadcasted_iota(jnp.int32, (TILE, 2 * TILE), 0)
+    cols_w = lax.broadcasted_iota(jnp.int32, (TILE, 2 * TILE), 1) & (TILE - 1)
+    for level in range(1, LEVELS + 1):
+        hit = ((rows_w ^ cols_w) >> level) == 1
+        masks[level - 1] = jnp.where(hit, 1.0, 0.0).astype(f32).astype(bf16)
+    starts = []
+    total = jnp.int32(0)
+    for s in range(lengths.shape[0]):
+        starts.append(total)
+        total = total + lengths[s]
+
+    def segment_of(position):
+        seg = jnp.zeros_like(position)
+        for s in starts:
+            seg = seg + jnp.where(position >= s, 1, 0)
+        return seg
+
+    def prepare(g, carry):
+        eye = jnp.where(rows == cols, 1.0, 0.0).astype(f32)
+        ramp = jnp.where(rows <= cols, 1.0, 0.0).astype(f32).astype(bf16)
+        near = (rows ^ cols) == 1
+        chains = []
+        for m in range(group):
+            c = g * group + m
+            q = x_ref[c, 0:TILE, :]
+            k = x_ref[c, TILE : 2 * TILE, :]
+            v = x_ref[c, 2 * TILE : 3 * TILE, :]
+            side = x_ref[c, 3 * TILE : 3 * TILE + SIDE, :]
+            k_t = k.astype(f32).T.astype(bf16)
+            both = mm(jnp.concatenate([q, k], axis=0), k_t)
+            qk, kk = both[:TILE], both[TILE:]
+            level = mm(side, ramp)
+            side32 = side.astype(f32)
+            b_row, g_row = side32[0:1], side32[1:2]
+            inc_row = level[1:2]
+            exc_row = inc_row - g_row
+            base = c * TILE
+            position = base + lax.broadcasted_iota(jnp.int32, (1, TILE), 1)
+            seg_row = segment_of(position).astype(f32)
+            before = segment_of(base - 1).astype(f32)
+            after = jnp.where(c == count - 1, -1, segment_of(base + TILE)).astype(f32)
+            stacked = jnp.concatenate(
+                [inc_row, exc_row, b_row, seg_row, jnp.zeros((4, TILE), f32)], axis=0
+            )
+            stacked_t = stacked.T
+            inc_col, exc_col = stacked_t[:, 0:1], stacked_t[:, 1:2]
+            b_col, seg_col = stacked_t[:, 2:3], stacked_t[:, 3:4]
+            diagonal = kk * eye
+            rn_row = 1.0 / jnp.sqrt(jnp.sum(diagonal, axis=0, keepdims=True) + 1e-06)
+            rn_col = 1.0 / jnp.sqrt(jnp.sum(diagonal, axis=1, keepdims=True) + 1e-06)
+            same = seg_col == seg_row
+            kk_b = kk * (rn_col * b_col) * rn_row
+            qk_n = qk * rn_row
+            last_inc = inc_row[:, TILE - 1 : TILE]
+            last_seg = seg_row[:, TILE - 1 : TILE]
+            first_seg = seg_row[:, 0:1]
+            v2 = jnp.concatenate([v, v], axis=0)
+            k2 = jnp.concatenate([k, k], axis=0)
+            kt2 = jnp.concatenate([k_t, k_t], axis=1)
+            q32 = q.astype(f32)
+            for direction in range(2):
+                if direction == 0:
+                    inside = same & (cols <= rows)
+                    strict = cols < rows
+                    gap = inc_col - inc_row
+                    c_row = jnp.where(seg_row == before, jnp.exp(inc_row), 0.0)
+                    c_col = jnp.where(seg_col == before, jnp.exp(inc_col), 0.0)
+                    w_col = jnp.where(seg_col == last_seg, jnp.exp(last_inc - inc_col), 0.0)
+                    c_last = c_row[:, TILE - 1 : TILE]
+                else:
+                    inside = same & (cols >= rows)
+                    strict = cols > rows
+                    gap = exc_row - exc_col
+                    c_row = jnp.where(seg_row == after, jnp.exp(last_inc - exc_row), 0.0)
+                    c_col = jnp.where(seg_col == after, jnp.exp(last_inc - exc_col), 0.0)
+                    w_col = jnp.where(seg_col == first_seg, jnp.exp(exc_col), 0.0)
+                    c_last = c_row[:, 0:1]
+                weight = jnp.where(inside, jnp.exp(jnp.where(inside, gap, 0.0)), 0.0)
+                lower = jnp.where(strict, weight * kk_b, 0.0)
+                scores = weight * qk_n
+                if direction == 1:
+                    scores = jnp.where(strict, scores, 0.0)
+                chains.append(
+                    dict(
+                        place=2 * c + direction,
+                        lower=wide(lower),
+                        inverse=eye - jnp.where(near, lower, 0.0),
+                        scores=halves(scores),
+                        b_row=b_row,
+                        bc_row=b_row * c_row * rn_row,
+                        wn_col=w_col * rn_col,
+                        c_last=c_last,
+                        cq=c_col * q32,
+                        v2=v2,
+                        k2=k2,
+                        kt2=kt2,
+                    )
+                )
+        for level in range(LEVELS):
+            mask = masks[level]
+            parts = [halves(n["inverse"]) for n in chains]
+            inner = [fold(mm(n["lower"] * mask, right(*p))) for n, p in zip(chains, parts)]
+            outer = [
+                fold(mm(jnp.concatenate(p, axis=1), right(*halves(y))))
+                for p, y in zip(parts, inner)
+            ]
+            for n, y in zip(chains, outer):
+                n["inverse"] = n["inverse"] - y
+        solved = [
+            jnp.concatenate(
+                [
+                    mm(wide(n["inverse"] * n["b_row"]), n["v2"]),
+                    mm(wide(n["inverse"] * n["bc_row"]), n["k2"]),
+                ],
+                axis=1,
+            )
+            for n in chains
+        ]
+        for n, u in zip(chains, solved):
+            u_h, u_l = halves(u)
+            s_h, s_l = n["scores"]
+            seen = mm(jnp.concatenate([s_h, s_l], axis=1), jnp.concatenate([u_h, u_h], axis=0))
+            seen = seen + mm(s_h, u_l)
+            kept = mm(n["kt2"], jnp.concatenate(halves(u * n["wn_col"]), axis=0))
+            effect = n["cq"] - seen[:, TILE:]
+            transit = n["c_last"] * eye - kept[:, TILE:]
+            fe[n["place"]] = wide(jnp.concatenate([transit, effect], axis=0))
+            go[n["place"]] = jnp.concatenate([kept[:, :TILE], seen[:, :TILE]], axis=0)
+        return carry
+
+    lax.fori_loop(0, count // group, prepare, 0)
+
+    def advance(step, states):
+        later = []
+        for direction, state in enumerate(states):
+            c = step if direction == 0 else count - 1 - step
+            place = 2 * c + direction
+            moved = fold(mm(fe[place], right(*halves(state)))) + go[place]
+            partial_out[place] = moved[TILE:]
+            later.append(moved[:TILE])
+        return tuple(later)
+
+    empty = jnp.zeros((TILE, TILE), f32)
+    lax.fori_loop(0, count, advance, (empty, empty))
+
+    def finish(c, carry):
+        out_ref[c] = (partial_out[2 * c] + partial_out[2 * c + 1]).astype(bf16)
+        return carry
+
+    lax.fori_loop(0, count, finish, 0)
+
+
+def mix_head(x, seg_lengths):
+    count = x.shape[0]
+    group = GROUP if count % GROUP == 0 else 1
+    return pl.pallas_call(
+        partial(mix_kernel, count, group),
+        out_shape=jax.ShapeDtypeStruct((count, TILE, DV), jnp.bfloat16),
+        in_specs=[
+            pl.BlockSpec(memory_space=pltpu.SMEM),
+            pl.BlockSpec(memory_space=pltpu.VMEM),
+        ],
+        out_specs=pl.BlockSpec(memory_space=pltpu.VMEM),
+        scratch_shapes=[
+            pltpu.VMEM((LEVELS, TILE, 2 * TILE), jnp.bfloat16),
+            pltpu.VMEM((2 * count, 2 * TILE, 2 * TILE), jnp.bfloat16),
+            pltpu.VMEM((2 * count, 2 * TILE, TILE), jnp.float32),
+            pltpu.VMEM((2 * count, TILE, TILE), jnp.float32),
+        ],
+        compiler_params=pltpu.CompilerParams(vmem_limit_bytes=52 * 1024 * 1024),
+        cost_estimate=pl.CostEstimate(
+            flops=count * 40 * TILE * 512 * 256, bytes_accessed=count * 131072, transcendentals=0
+        ),
+    )(seg_lengths, x)
+
+
+def one_head_each(queries, keys, values, beta, log_decay, seg_lengths):
+    axes = ("seq", "head")
+    tokens = queries.shape[0]
+    heads = beta.shape[1]
+
+    def by_head(array):
+        return array.reshape(tokens, heads, TILE).transpose(1, 0, 2)
+
+    side = jnp.stack([beta.T, log_decay.T], axis=1)
+    side = jnp.pad(side, ((0, 0), (0, SIDE - 2), (0, 0)))
+    packed = jnp.concatenate([by_head(queries), by_head(keys), by_head(values), side], axis=1)
+    x = lax.all_to_all(packed, axes, split_axis=0, concat_axis=0, tiled=True)
+    mixed = mix_head(x, seg_lengths)
+    back = lax.all_to_all(mixed, axes, split_axis=0, concat_axis=0, tiled=True)
+    return back.transpose(1, 0, 2).reshape(tokens, heads * DV)
 
 
 def span_parts(query_rows, key_rows, value_rows, write_rate, log_gate, reset_flags, inclusive):
@@ -200,6 +426,16 @@
         P(),
     )
     out_specs = P(("seq", "head"), None)
-    return jax.shard_map(
-        on_device, mesh=mesh, in_specs=in_specs, out_specs=out_specs, check_vma=False
-    )
+    devices = mesh.shape["seq"] * mesh.shape["head"]
+
+    def run(queries, keys, values, beta, log_decay, seg_lengths):
+        alone = beta.shape[1] == devices and queries.shape[0] == devices * TILE
+        return jax.shard_map(
+            one_head_each if alone else on_device,
+            mesh=mesh,
+            in_specs=in_specs,
+            out_specs=out_specs,
+            check_vma=False,
+        )(queries, keys, values, beta, log_decay, seg_lengths)
+
+    return run

time: 1100 us -> 169 us (0.15)
  other arithmetic: 650 us -> 0.33 us
  matrix products: 224 us -> 0 us
  local copies, waits for them, and re-layouts: 101 us -> 11.8 us
  blocking collectives: 27.5 us -> 110 us
  waiting for transfers between devices: 49.4 us -> 0 us
  Pallas kernels: 0 us -> 45.6 us
  starting transfers between devices: 22.5 us -> 0 us
  between operations: 14.1 us -> 0.09 us
    another operation x9 -> x1, other arithmetic: 637 us -> 0.06 us  [one_head_each(): side = jnp.stack([beta.T, log_decay.T], axis=1)]
    dot_general x92 -> x0, matrix products: 216 us -> none  [the longest x16 29.6 us: step(): jnp.einsum('hvj,hjk->hvk', carry, transit_step, precision=highest)]
    all_to_all x1 -> x2, blocking collectives: 27.5 us -> 110 us  [the longest x1 82.3 us: one_head_each(): x = lax.all_to_all(packed, axes, split_axis=0, concat_axis=0, tiled=True)]
    all_to_all x5 -> x0, waiting for transfers between devices: 49.3 us -> none  [the longest x1 24.7 us: on_device(): lax.all_to_all(queries, 'head', split_axis=1, concat_axis=0, tiled=True)]
    pallas_call x0 -> x1, Pallas kernels: none -> 45.6 us  [mix_head(): pl.pallas_call(partial(mix_kernel, count, group), out_shape=jax.ShapeDtyp...]
    unnamed x49 -> x5, local copies, waits for them, and re-layouts: 34.7 us -> 5.5 us
    rev x10 -> x0, local copies, waits for them, and re-layouts: 25.3 us -> none  [the longest x1 10.2 us: on_device(): emit(backward_pieces[0], backward_pieces[1], backward_pieces[2], backward...]
    all_to_all x5 -> x0, starting transfers between devices: 22.3 us -> none  [the longest x1 6.32 us: on_device(): lax.all_to_all(log_decay, 'head', split_axis=1, concat_axis=0, tiled=True)]
  transfers between devices with their start and end apart: 9 -> 0, of which waited for: 4 -> 0; matrix products, arithmetic and copies ran while one was open for 76% -> 0% of each run, Pallas kernels for 0% -> 0%
where the time goes in v1:
time: 169 us; the launch traced here: 167 us
  blocking collectives  110 us (65%)
  Pallas kernels  45.6 us (27%)
  local copies, waits for them, and re-layouts  11.8 us (7%)
    all_to_all x1, blocking collectives, one_head_each(): x = lax.all_to_all(packed, axes, split_axis=0, concat_axis=0, tiled=True)  82.3 us
    pallas_call x1, Pallas kernels, mix_head(): pl.pallas_call(partial(mix_kernel, count, group), out_shape=jax.ShapeDtyp...  45.6 us
    all_to_all x1, blocking collectives, one_head_each(): back = lax.all_to_all(mixed, axes, split_axis=0, concat_axis=0, tiled=True)  27.4 us
    unnamed x5, local copies, waits for them, and re-layouts  5.5 us

profile of v1, /device:TPU:0, one launch (start us, length us, event | category | flops | bytes accessed | tf_op | source)
XLA Modules:
  0.0 167.5 jit_solution(16263000683326447727)
XLA Ops:
  0.0 0.7 copy.13
  0.7 0.7 copy.14
  1.4 1.6 copy.7
  3.1 0.7 copy.8
  3.7 1.6 copy.9
  5.4 0.7 copy.10
  6.0 2.3 %copy.11 = bf16[128,4096]{0,1:T(8,128)(2,1)} copy(bf16[128,4096]{1,0:T(8,128)(2,1)} %param.8) | data formatting | bytes 2097152 | tf_op args[2]
  8.3 1.6 copy.12
  9.9 0.1 fusion.2
  10.0 0.3 pad_maximum_fusion
  10.3 0.0 copy-start
  10.3 82.3 %all_to_all.10.x_ref = bf16[32,400,128]{2,1,0:T(8,128)(2,1)} all-to-all(bf16[32,400,128]{2,1,0:T(8,128)(2,1)S(1)} %pad_maximum_fusion), channel_id=1, replica_groups=mesh['seq'=8,'head'=4] {'seq','head'}, dimensions={0} | all-to-all | bytes 6553600 | tf_op jit(solution)/shard_map/all_to_all | solution.py:233
  92.5 0.0 copy-done
  92.5 45.6 %shard_map.64 = bf16[32,128,128]{2,1,0:T(8,128)(2,1)S(1)} custom-call(s32[8]{0:T(128)S(1)} %copy-done, bf16[32,400,128]{2,1,0:T(8,128)(2,1)} %all_to_all.10.x_ref), custom_call_target="tpu_custom_call" | custom-call | flops 21474836480 | bytes 4194304 | tf_op jit(solution)/shard_map/pallas_call | solution.py:201
  138.1 27.4 %all_to_all.11 = bf16[32,128,128]{2,1,0:T(8,128)(2,1)S(1)} all-to-all(bf16[32,128,128]{2,1,0:T(8,128)(2,1)S(1)} %shard_map.64), channel_id=1, replica_groups=mesh['seq'=8,'head'=4] {'seq','head'}, dimensions={0} | all-to-all | bytes 2097152 | tf_op jit(solution)/shard_map/all_to_all | solution.py:235
  165.5 0.7 copy.15
  166.2 1.3 copy.16
Async XLA Ops:
  10.3 82.3 %copy-start = (s32[8]{0:T(128)S(1)}, s32[8]{0:T(128)}, u32[]{:S(2)}) copy-start(s32[8]{0:T(128)} %lengths.1) | copy-start | bytes 100

commit v2 on v1

--- a/solution.py
+++ b/solution.py
@@ -39,7 +39,88 @@
     return a[:, :TILE] + a[:, TILE:]
 
 
-def mix_kernel(count, group, lengths, x_ref, out_ref, masks, fe, go, partial_out):
+def mix_kernel(
+    spread,
+    inner,
+    group,
+    lengths,
+    side_ref,
+    q_ref,
+    k_ref,
+    v_ref,
+    out_ref,
+    q_all,
+    k_all,
+    v_all,
+    side_all,
+    masks,
+    fe,
+    go,
+    partial_out,
+    mixed,
+    own_sem,
+    send_sem,
+    recv_sem,
+    back_send,
+    back_recv,
+):
+    count = spread * inner
+    me = lax.axis_index("seq") * inner + lax.axis_index("head")
+
+    def device(index):
+        return (index // inner, index % inner)
+
+    def columns(index):
+        return pl.ds(pl.multiple_of(index * TILE, TILE), TILE)
+
+    barrier = pltpu.get_barrier_semaphore()
+
+    def greet(s, carry):
+        pl.semaphore_signal(
+            barrier,
+            inc=1,
+            device_id=device((me + s) % count),
+            device_id_type=pl.DeviceIdType.MESH,
+        )
+        return carry
+
+    lax.fori_loop(1, count, greet, 0)
+    pl.semaphore_wait(barrier, count - 1)
+
+    def pairs(head, block):
+        return (
+            (side_ref.at[head], side_all.at[block]),
+            (k_ref.at[:, columns(head)], k_all.at[block]),
+            (v_ref.at[:, columns(head)], v_all.at[block]),
+            (q_ref.at[:, columns(head)], q_all.at[block]),
+        )
+
+    def sends(target, source):
+        return [
+            pltpu.make_async_remote_copy(
+                src_ref=src,
+                dst_ref=dst,
+                send_sem=send_sem.at[kind, target],
+                recv_sem=recv_sem.at[kind, source],
+                device_id=device(target),
+                device_id_type=pl.DeviceIdType.MESH,
+            )
+            for kind, (src, dst) in enumerate(pairs(target, source))
+        ]
+
+    def give(s, carry):
+        for copy in sends((me + s) % count, me):
+            copy.start()
+        return carry
+
+    lax.fori_loop(1, count, give, 0)
+    own = [
+        pltpu.make_async_copy(src, dst, own_sem.at[kind])
+        for kind, (src, dst) in enumerate(pairs(me, me))
+    ]
+    for copy in own:
+        copy.start()
+
     bf16, f32 = jnp.bfloat16, jnp.float32
     rows = lax.broadcasted_iota(jnp.int32, (TILE, TILE), 0)
     cols = lax.broadcasted_iota(jnp.int32, (TILE, TILE), 1)
@@ -60,17 +141,26 @@
             seg = seg + jnp.where(position >= s, 1, 0)
         return seg
 
+    for copy in own:
+        copy.wait()
+
     def prepare(g, carry):
+        for m in range(group):
+            s = g * group + m
+
+            @pl.when(s > 0)
+            def _():
+                source = (me + count - s) % count
+                for copy in sends(source, source):
+                    copy.wait_recv()
+
         eye = jnp.where(rows == cols, 1.0, 0.0).astype(f32)
         ramp = jnp.where(rows <= cols, 1.0, 0.0).astype(f32).astype(bf16)
         near = (rows ^ cols) == 1
         chains = []
         for m in range(group):
-            c = g * group + m
-            q = x_ref[c, 0:TILE, :]
-            k = x_ref[c, TILE : 2 * TILE, :]
-            v = x_ref[c, 2 * TILE : 3 * TILE, :]
-            side = x_ref[c, 3 * TILE : 3 * TILE + SIDE, :]
+            c = (me + count - (g * group + m)) % count
+            q, k, v, side = q_all[c], k_all[c], v_all[c], side_all[c]
             k_t = k.astype(f32).T.astype(bf16)
             both = mm(jnp.concatenate([q, k], axis=0), k_t)
             qk, kk = both[:TILE], both[TILE:]
@@ -175,65 +265,89 @@
 
     lax.fori_loop(0, count // group, prepare, 0)
 
-    def advance(step, states):
-        later = []
-        for direction, state in enumerate(states):
-            c = step if direction == 0 else count - 1 - step
-            place = 2 * c + direction
-            moved = fold(mm(fe[place], right(*halves(state)))) + go[place]
-            partial_out[place] = moved[TILE:]
-            later.append(moved[:TILE])
-        return tuple(later)
+    def advance(turn, states):
+        for m in range(group):
+            step = turn * group + m
+            later = []
+            for direction, state in enumerate(states):
+                c = step if direction == 0 else count - 1 - step
+                place = 2 * c + direction
+                moved = fold(mm(fe[place], right(*halves(state)))) + go[place]
+                partial_out[place] = moved[TILE:]
+                later.append(moved[:TILE])
+            states = tuple(later)
+        return states
 
     empty = jnp.zeros((TILE, TILE), f32)
-    lax.fori_loop(0, count, advance, (empty, empty))
-
-    def finish(c, carry):
-        out_ref[c] = (partial_out[2 * c] + partial_out[2 * c + 1]).astype(bf16)
+    lax.fori_loop(0, count // group, advance, (empty, empty))
+
+    def returns(target, source):
+        return pltpu.make_async_remote_copy(
+            src_ref=mixed.at[target],
+            dst_ref=out_ref.at[:, columns(source)],
+            send_sem=back_send.at[target],
+            recv_sem=back_recv.at[source],
+            device_id=device(target),
+            device_id_type=pl.DeviceIdType.MESH,
+        )
+
+    def finish(s, carry):
+        c = (me + s) % count
+        mixed[c] = (partial_out[2 * c] + partial_out[2 * c + 1]).astype(bf16)
+        returns(c, me).start()
         return carry
 
-    lax.fori_loop(0, count, finish, 0)
-
-
-def mix_head(x, seg_lengths):
-    count = x.shape[0]
+    lax.fori_loop(1, count, finish, 0)
+    out_ref[:, columns(me)] = (partial_out[2 * me] + partial_out[2 * me + 1]).astype(bf16)
+
+    def settle(s, carry):
+        target = (me + s) % count
+        for copy in sends(target, me):
+            copy.wait_send()
+        returns(target, me).wait_send()
+        source = (me + count - s) % count
+        returns(source, source).wait_recv()
+        return carry
+
+    lax.fori_loop(1, count, settle, 0)
+
+
+def one_head_each(queries, keys, values, beta, log_decay, seg_lengths):
+    spread, inner = lax.axis_size("seq"), lax.axis_size("head")
+    count = spread * inner
     group = GROUP if count % GROUP == 0 else 1
+    side = jnp.stack([beta.T, log_decay.T], axis=1)
+    side = jnp.pad(side, ((0, 0), (0, SIDE - 2), (0, 0)))
     return pl.pallas_call(
-        partial(mix_kernel, count, group),
-        out_shape=jax.ShapeDtypeStruct((count, TILE, DV), jnp.bfloat16),
-        in_specs=[
-            pl.BlockSpec(memory_space=pltpu.SMEM),
-            pl.BlockSpec(memory_space=pltpu.VMEM),
-        ],
+        partial(mix_kernel, spread, inner, group),
+        out_shape=jax.ShapeDtypeStruct((TILE, count * DV), jnp.bfloat16),
+        in_specs=[pl.BlockSpec(memory_space=pltpu.SMEM)]
+        + [pl.BlockSpec(memory_space=pltpu.VMEM)]
+        + [pl.BlockSpec(memory_space=pl.ANY)] * 3,
         out_specs=pl.BlockSpec(memory_space=pltpu.VMEM),
         scratch_shapes=[
+            pltpu.VMEM((count, TILE, DK), jnp.bfloat16),
+            pltpu.VMEM((count, TILE, DK), jnp.bfloat16),
+            pltpu.VMEM((count, TILE, DV), jnp.bfloat16),
+            pltpu.VMEM((count, SIDE, TILE), jnp.bfloat16),
             pltpu.VMEM((LEVELS, TILE, 2 * TILE), jnp.bfloat16),
             pltpu.VMEM((2 * count, 2 * TILE, 2 * TILE), jnp.bfloat16),
             pltpu.VMEM((2 * count, 2 * TILE, TILE), jnp.float32),
             pltpu.VMEM((2 * count, TILE, TILE), jnp.float32),
+            pltpu.VMEM((count, TILE, DV), jnp.bfloat16),
+            pltpu.SemaphoreType.DMA((4,)),
+            pltpu.SemaphoreType.DMA((4, count)),
+            pltpu.SemaphoreType.DMA((4, count)),
+            pltpu.SemaphoreType.DMA((count,)),
+            pltpu.SemaphoreType.DMA((count,)),
         ],
-        compiler_params=pltpu.CompilerParams(vmem_limit_bytes=52 * 1024 * 1024),
+        compiler_params=pltpu.CompilerParams(
+            collective_id=0, has_side_effects=True, vmem_limit_bytes=52 * 1024 * 1024
+        ),
         cost_estimate=pl.CostEstimate(
             flops=count * 40 * TILE * 512 * 256, bytes_accessed=count * 131072, transcendentals=0
         ),
-    )(seg_lengths, x)
-
-
-def one_head_each(queries, keys, values, beta, log_decay, seg_lengths):
-    axes = ("seq", "head")
-    tokens = queries.shape[0]
-    heads = beta.shape[1]
-
-    def by_head(array):
-        return array.reshape(tokens, heads, TILE).transpose(1, 0, 2)
-
-    side = jnp.stack([beta.T, log_decay.T], axis=1)
-    side = jnp.pad(side, ((0, 0), (0, SIDE - 2), (0, 0)))
-    packed = jnp.concatenate([by_head(queries), by_head(keys), by_head(values), side], axis=1)
-    x = lax.all_to_all(packed, axes, split_axis=0, concat_axis=0, tiled=True)
-    mixed = mix_head(x, seg_lengths)
-    back = lax.all_to_all(mixed, axes, split_axis=0, concat_axis=0, tiled=True)
-    return back.transpose(1, 0, 2).reshape(tokens, heads * DV)
+    )(seg_lengths, side, queries, keys, values)
 
 
 def span_parts(query_rows, key_rows, value_rows, write_rate, log_gate, reset_flags, inclusive):

time: 169 us -> 119 us (0.70)
  blocking collectives: 110 us -> 0 us
  Pallas kernels: 45.6 us -> 116 us
  local copies, waits for them, and re-layouts: 11.8 us -> 2.3 us
    all_to_all x2 -> x0, blocking collectives: 110 us -> none  [the longest x1 82.3 us: one_head_each(): x = lax.all_to_all(packed, axes, split_axis=0, concat_axis=0, tiled=True)]
    pallas_call x1, Pallas kernels: 45.6 us -> 116 us  [one_head_each(): pl.pallas_call(partial(mix_kernel, spread, inner, group), out_shape=jax.S...]
    reshape x4 -> x0, local copies, waits for them, and re-layouts: 4.26 us -> none  [the longest x3 2.94 us: by_head(): return array.reshape(tokens, heads, TILE).transpose(1, 0, 2)]
    unnamed x5, local copies, waits for them, and re-layouts: 5.5 us -> 1.56 us
where the time goes in v2:
time: 119 us
  Pallas kernels  116 us (97%)
  local copies, waits for them, and re-layouts  2.3 us (2%)
    pallas_call x1, Pallas kernels, one_head_each(): pl.pallas_call(partial(mix_kernel, spread, inner, group), out_shape=jax.S...  116 us

profile of v2, /device:TPU:0, one launch (start us, length us, event | category | flops | bytes accessed | tf_op | source)
XLA Modules:
  0.0 118.7 jit_solution(4163116998701322530)
XLA Ops:
  0.0 0.0 copy-start.1
  0.0 0.7 copy.7
  0.7 0.0 copy-done.1
  0.8 0.0 copy-start
  0.8 0.1 fusion.2.side_ref
  0.8 0.6 copy-done
  1.4 116.3 %shard_map.64 = bf16[128,4096]{1,0:T(8,128)(2,1)S(1)} custom-call(s32[8]{0:T(128)S(1)} %copy-done, bf16[32,16,128]{2,1,0:T(8,128)(2,1)S(1)} %fusion.2.side_ref, bf16[128,4096]{1,0:T(8,128)(2,1)} %q_ref.1, bf16[128,4096]{1,0:T(8,128)(2,1)} %k_ref.1, bf16[128,4096]{1,0:T(8,128)(2,1)} %v_ref.1), custom_call_target="tpu_custom_call" | custom-call | flops 21474836480 | bytes 4194304 | tf_op jit(solution)/shard_map/pallas_call | solution.py:321
  117.8 1.0 copy.10
  (1 shorter events, 0.0 us)
Async XLA Ops:
  0.0 0.7 copy-start.1
  0.8 0.7 copy-start

commit v3 on v2

--- a/solution.py
+++ b/solution.py
@@ -160,13 +160,12 @@
         chains = []
         for m in range(group):
             c = (me + count - (g * group + m)) % count
-            q, k, v, side = q_all[c], k_all[c], v_all[c], side_all[c]
+            q, k, v, side32 = q_all[c], k_all[c], v_all[c], side_all[c]
             k_t = k.astype(f32).T.astype(bf16)
             both = mm(jnp.concatenate([q, k], axis=0), k_t)
             qk, kk = both[:TILE], both[TILE:]
-            level = mm(side, ramp)
-            side32 = side.astype(f32)
             b_row, g_row = side32[0:1], side32[1:2]
+            level = mm(jnp.concatenate([side32] * (SIDE // 2), axis=0).astype(bf16), ramp)
             inc_row = level[1:2]
             exc_row = inc_row - g_row
             base = c * TILE
@@ -317,7 +316,7 @@
     count = spread * inner
     group = GROUP if count % GROUP == 0 else 1
     side = jnp.stack([beta.T, log_decay.T], axis=1)
-    side = jnp.pad(side, ((0, 0), (0, SIDE - 2), (0, 0)))
+    side = side.astype(jnp.float32)
     return pl.pallas_call(
         partial(mix_kernel, spread, inner, group),
         out_shape=jax.ShapeDtypeStruct((TILE, count * DV), jnp.bfloat16),
@@ -329,7 +328,7 @@
             pltpu.VMEM((count, TILE, DK), jnp.bfloat16),
             pltpu.VMEM((count, TILE, DK), jnp.bfloat16),
             pltpu.VMEM((count, TILE, DV), jnp.bfloat16),
-            pltpu.VMEM((count, SIDE, TILE), jnp.bfloat16),
+            pltpu.VMEM((count, 2, TILE), jnp.float32),
             pltpu.VMEM((LEVELS, TILE, 2 * TILE), jnp.bfloat16),
             pltpu.VMEM((2 * count, 2 * TILE, 2 * TILE), jnp.bfloat16),
             pltpu.VMEM((2 * count, 2 * TILE, TILE), jnp.float32),

time: 119 us -> 117 us (0.983)
    pallas_call x1, Pallas kernels: 116 us -> 115 us  [one_head_each(): pl.pallas_call(partial(mix_kernel, spread, inner, group), out_shape=jax.S...]
where the time goes in v3:
time: 117 us
  Pallas kernels  115 us (98%)
  local copies, waits for them, and re-layouts  2.31 us (2%)
    pallas_call x1, Pallas kernels, one_head_each(): pl.pallas_call(partial(mix_kernel, spread, inner, group), out_shape=jax.S...  115 us

profile of v3, /device:TPU:0, one launch (start us, length us, event | category | flops | bytes accessed | tf_op | source)
XLA Modules:
  0.0 117.0 jit_solution(7218122394969279252)
XLA Ops:
  0.0 0.0 copy-start.1
  0.0 0.7 copy.7
  0.7 0.0 copy-done.1
  0.8 0.0 copy-start
  0.8 0.6 copy-done
  1.4 114.6 %shard_map.64 = bf16[128,4096]{1,0:T(8,128)(2,1)S(1)} custom-call(s32[8]{0:T(128)S(1)} %copy-done, f32[32,2,128]{2,1,0:T(2,128)S(1)} %maximum_convert_fusion.side_ref, bf16[128,4096]{1,0:T(8,128)(2,1)} %q_ref.1, bf16[128,4096]{1,0:T(8,128)(2,1)} %k_ref.1, bf16[128,4096]{1,0:T(8,128)(2,1)} %v_ref.1), custom_call_target="tpu_custom_call" | custom-call | flops 21474836480 | bytes 4194304 | tf_op jit(solution)/shard_map/pallas_call | solution.py:320
  116.0 1.0 copy.10
  (2 shorter events, 0.1 us)
Async XLA Ops:
  0.0 0.7 copy-start.1
  0.8 0.7 copy-start
